TPU v7x, 32 devices: a whole 2x2x4 slice. The times are simulated.
32 devices in a mesh: dom: 2 (over x), gy: 4 (over y, core), gz: 4 (over z).
Axes of the slice: x: 2, y: 2, z: 4, core: 2. Of those that a mesh axis runs over, the one named last changes fastest.
Arguments:
- right_side: float32 [32, 256, 512], P('dom', 'gy', 'gz'), may hold values from -8 to 8
- coefficient: float32 [32, 256, 512], P('dom', 'gy', 'gz'), may hold values from 0.1 to 10
Outputs:
- solution: float32 [32, 256, 512], P('dom', 'gy', 'gz')
- residual: float32 [32, 256, 512], P('dom', 'gy', 'gz')
All inputs are finite; a program needn't handle non-finite values.
Results may differ from a plain program's by a relative error of at most 0.00028.
Values sent between devices are 32-bit elements; how exact they have to be, the bound alone decides.
A program may use at most 128 MiB of HBM per device.

v0:
```python
import jax
import jax.numpy as jnp
from jax import lax
from jax.sharding import PartitionSpec as P

LEVELS = 4
NU = 2
COARSE_SWEEPS = 8


OMEGA = 0.8


def extended(shard, sides, width):
    for axis, dim in sides:
        peers, length = (lax.axis_size(axis), shard.shape[dim])
        up = [(i, (i + 1) % peers) for i in range(peers - 1)]
        down = [(j, i) for i, j in up]
        last = lax.slice_in_dim(shard, length - width, length, axis=dim)
        initial = lax.slice_in_dim(shard, 0, width, axis=dim)
        before = lax.ppermute(last, axis, up)
        after = lax.ppermute(initial, axis, down)
        shard = jnp.concatenate([before, shard, after], axis=dim)
    return shard


def neighbours(padded):
    return (
        padded[2:, 1:-1, 1:-1],
        padded[:-2, 1:-1, 1:-1],
        padded[1:-1, 2:, 1:-1],
        padded[1:-1, :-2, 1:-1],
        padded[1:-1, 1:-1, 2:],
        padded[1:-1, 1:-1, :-2],
    )


def face_weights(coefficient, padded_coefficient):
    result = []
    for beside in neighbours(padded_coefficient):
        result.append(0.5 * (coefficient + beside))
    summed = result[0]
    for weight in result[1:]:
        summed = summed + weight
    return (tuple(result), summed)


def apply_operator(iterate, padded_iterate, weights):
    summed = jnp.zeros_like(iterate)
    for weight, beside in zip(weights, neighbours(padded_iterate)):
        summed = summed + weight * (iterate - beside)
    return summed


def coarsen_sum(values):
    size_x, size_y, size_z = values.shape
    return values.reshape(size_x // 2, 2, size_y // 2, 2, size_z // 2, 2).sum(axis=(1, 3, 5))


def prolong(values):
    return jnp.repeat(jnp.repeat(jnp.repeat(values, 2, 0), 2, 1), 2, 2)


def pad_grid(values):
    return extended(values, (("dom", 0), ("gy", 1), ("gz", 2)), 1)


def prepare(coefficient):
    padded = extended(coefficient, (("dom", 0), ("gy", 1), ("gz", 2)), 1)
    return face_weights(coefficient, padded)


def image_level(iterate, prepared):
    weights, diagonal = prepared
    return (apply_operator(iterate, pad_grid(iterate), weights), diagonal)


def smooth_level(iterate, source, prepared, sweeps, from_zero):
    for sweep_index in range(sweeps):
        if prepared is not None and from_zero and (sweep_index == 0):
            iterate = OMEGA * source / prepared[1]
        else:
            applied, diagonal = image_level(iterate, prepared)
            iterate = iterate + OMEGA * (source - applied) / diagonal
    return iterate


def body(right_side, coefficient):
    sources = [right_side]
    coefficients = [coefficient]
    operators = []
    smoothed = []
    spread_levels = LEVELS
    for level_index in range(spread_levels):
        prepared = prepare(coefficients[-1])
        operators.append(prepared)
        iterate = smooth_level(jnp.zeros_like(sources[-1]), sources[-1], prepared, NU, True)
        smoothed.append(iterate)
        applied, diagonal = image_level(iterate, prepared)
        sources.append(0.5 * coarsen_sum(sources[-1] - applied))
        coefficients.append(0.125 * coarsen_sum(coefficients[-1]))
    prepared = prepare(coefficients[-1])
    correction = smooth_level(
        jnp.zeros_like(sources[-1]), sources[-1], prepared, COARSE_SWEEPS, True
    )
    for level_index in range(spread_levels - 1, -1, -1):
        iterate = smoothed[level_index] + prolong(correction)
        correction = smooth_level(iterate, sources[level_index], operators[level_index], NU, False)
    applied, diagonal = image_level(correction, operators[0])
    return (correction, right_side - applied)


def solution(mesh):
    in_specs = (P("dom", "gy", "gz"), P("dom", "gy", "gz"))
    out_specs = (P("dom", "gy", "gz"), P("dom", "gy", "gz"))
    return jax.shard_map(body, mesh=mesh, in_specs=in_specs, out_specs=out_specs, check_vma=False)
```

profile of v0, /device:TPU:1, one launch (start us, length us, event | category | flops | bytes accessed | tf_op | source)
XLA Modules:
  0.0 924.7 jit_solution(14254599394503451074)
XLA Ops:
  6.7 35.6 %reshape.95 = f32[8,2,32,2,64,2]{5,4,3,2,1,0:T(8,128)} reshape(f32[16,64,128]{2,1,0:T(8,128)} %param.3) | data formatting | bytes 1048576 | tf_op jit(solution)/shard_map/reshape | solution.py:57
  42.3 12.3 %reduce_sum.87 = f32[8,32,64]{2,1,0:T(8,128)S(1)} reduce(f32[8,2,32,2,64,2]{5,4,3,2,1,0:T(8,128)} %reshape.95, f32[]{:T(128)} %constant.7.clone.1), dimensions={1,3,5}, to_apply=%region_1.0 | reduce | flops 114688 | bytes 589828 | tf_op jit(solution)/shard_map/reduce_sum | solution.py:57
  79.6 6.4 fusion.83
  102.6 4.8 collective-permute-start.9
  122.9 5.5 collective-permute-start.11
  135.7 6.1 fusion.68
  143.5 4.9 collective-permute-start.13
  156.3 5.3 collective-permute-start.15
  176.6 4.8 collective-permute-start.17
  188.6 7.1 fusion.51
  198.2 35.6 %reshape.94 = f32[8,2,32,2,64,2]{5,4,3,2,1,0:T(8,128)} reshape(f32[16,64,128]{2,1,0:T(8,128)} %copy.205) | data formatting | bytes 1048576 | tf_op jit(solution)/shard_map/reshape | solution.py:57
  233.8 12.2 %reduce_sum.86 = f32[8,32,64]{2,1,0:T(8,128)S(1)} reduce(f32[8,2,32,2,64,2]{5,4,3,2,1,0:T(8,128)} %reshape.94, f32[]{:T(128)} %constant.7.clone.1), dimensions={1,3,5}, to_apply=%region_0.0 | reduce | flops 114688 | bytes 589828 | tf_op jit(solution)/shard_map/reduce_sum | solution.py:57
  254.3 5.7 mul.727
  264.0 4.8 collective-permute-start.27
  276.7 5.0 collective-permute-start.29
  282.3 5.4 collective-permute-start.37
  327.1 6.6 reshape.96
  358.5 5.5 collective-permute-start.47
  431.4 4.9 collective-permute-start.65
  447.8 5.1 collective-permute-start.69
  477.1 6.1 collective-permute-start.81
  830.6 6.1 fusion.37
  872.6 6.1 fusion.20
  914.6 7.3 fusion.3
  (660 shorter events, 711.4 us)
Async XLA Ops:
  1.4 53.1 %collective-permute-start.1 = (f32[1,64,128]{2,1,0:T(8,128)S(1)}, f32[1,64,128]{2,1,0:T(8,128)S(1)}, u32[]{:S(2)}, u32[]{:S(2)}) collective-permute-start(f32[1,64,128]{2,1,0:T(8,128)S(1)} %get-tuple-element.87), channel_id=1, source_target_pairs={{0,16},{1,17},{2,18},{3,19},{4,20},{5,21},{6,22},{7,23},{8,24},{9,... | collective-permute-start | bytes 98312 | tf_op jit(solution)/shard_map/ppermute | solution.py:21
  5.4 49.2 %collective-permute-start = (f32[1,64,128]{2,1,0:T(8,128)S(1)}, f32[1,64,128]{2,1,0:T(8,128)S(1)}, u32[]{:S(2)}, u32[]{:S(2)}) collective-permute-start(f32[1,64,128]{2,1,0:T(8,128)S(1)} %get-tuple-element.86), channel_id=1, source_target_pairs={{16,0},{17,1},{18,2},{19,3},{20,4},{21,5},{22,6},{23,7},{24,8},{25... | collective-permute-start | bytes 98312 | tf_op jit(solution)/shard_map/ppermute | solution.py:22
  87.7 13.9 %collective-permute-start.7 = (f32[1,64,128]{1,0,2:T(1,128)}, f32[1,64,128]{1,0,2:T(1,128)S(1)}, u32[]{:S(2)}, u32[]{:S(2)}) collective-permute-start(f32[1,64,128]{1,0,2:T(1,128)} %get-tuple-element.57), channel_id=1, source_target_pairs={{0,16},{1,17},{2,18},{3,19},{4,20},{5,21},{6,22},{7,23},{8,24},{9,... | collective-permute-start | bytes 98312 | tf_op jit(solution)/shard_map/ppermute | solution.py:21
  93.9 15.5 %collective-permute-start.19 = (f32[1,32,64]{2,1,0:T(8,128)}, f32[1,32,64]{2,1,0:T(8,128)S(1)}, u32[]{:S(2)}, u32[]{:S(2)}) collective-permute-start(f32[1,32,64]{2,1,0:T(8,128)} %get-tuple-element.116), channel_id=1, source_target_pairs={{0,16},{1,17},{2,18},{3,19},{4,20},{5,21},{6,22},{7,23},{8,24},{9,... | collective-permute-start | bytes 24584 | tf_op jit(solution)/shard_map/ppermute | solution.py:21
  102.6 12.9 %collective-permute-start.9 = (f32[18,1,128]{2,1,0:T(1,128)S(1)}, f32[18,1,128]{2,1,0:T(1,128)S(1)}, u32[]{:S(2)}, u32[]{:S(2)}) collective-permute-start(f32[18,1,128]{2,1,0:T(1,128)S(1)} %get-tuple-element.77), channel_id=1, source_target_pairs={{0,4},{4,8},{8,12},{1,5},{5,9},{9,13},{2,6},{6,10},{10,14},{3,7},{... | collective-permute-start | bytes 27656 | tf_op jit(solution)/shard_map/ppermute | solution.py:21
  110.0 39.7 %collective-permute-start.21 = (f32[10,1,64]{2,1,0:T(1,128)}, f32[10,1,64]{2,1,0:T(1,128)S(1)}, u32[]{:S(2)}, u32[]{:S(2)}) collective-permute-start(f32[10,1,64]{2,1,0:T(1,128)} %get-tuple-element.106), channel_id=1, source_target_pairs={{0,4},{4,8},{8,12},{1,5},{5,9},{9,13},{2,6},{6,10},{10,14},{3,7},{... | collective-permute-start | bytes 7688 | tf_op jit(solution)/shard_map/ppermute | solution.py:21
  113.6 36.1 %collective-permute-start.20 = (f32[10,1,64]{2,1,0:T(1,128)}, f32[10,1,64]{2,1,0:T(1,128)}, u32[]{:S(2)}, u32[]{:S(2)}) collective-permute-start(f32[10,1,64]{2,1,0:T(1,128)} %get-tuple-element.107), channel_id=1, source_target_pairs={{4,0},{8,4},{12,8},{5,1},{9,5},{13,9},{6,2},{10,6},{14,10},{7,3},{... | collective-permute-start | bytes 7688 | tf_op jit(solution)/shard_map/ppermute | solution.py:22
  121.6 14.1 %collective-permute-start.10 = (f32[18,66,1]{1,0,2:T(8,128)}, f32[18,66,1]{1,0,2:T(8,128)S(1)}, u32[]{:S(2)}, u32[]{:S(2)}) collective-permute-start(f32[18,66,1]{1,0,2:T(8,128)} %get-tuple-element.45), channel_id=1, source_target_pairs={{1,0},{2,1},{3,2},{5,4},{6,5},{7,6},{9,8},{10,9},{11,10},{13,12},{... | collective-permute-start | bytes 14264 | tf_op jit(solution)/shard_map/ppermute | solution.py:22
  156.3 13.2 %collective-permute-start.15 = (f32[18,1,128]{2,1,0:T(1,128)S(1)}, f32[18,1,128]{2,1,0:T(1,128)S(1)}, u32[]{:S(2)}, u32[]{:S(2)}) collective-permute-start(f32[18,1,128]{2,1,0:T(1,128)S(1)} %get-tuple-element.73), channel_id=1, source_target_pairs={{0,4},{4,8},{8,12},{1,5},{5,9},{9,13},{2,6},{6,10},{10,14},{3,7},{... | collective-permute-start | bytes 27656 | tf_op jit(solution)/shard_map/ppermute | solution.py:21
  164.3 81.7 %collective-permute-start.23 = (f32[10,34,1]{2,1,0:T(8,128)}, f32[10,34,1]{2,1,0:T(8,128)}, u32[]{:S(2)}, u32[]{:S(2)}) collective-permute-start(f32[10,34,1]{2,1,0:T(8,128)} %get-tuple-element.96), channel_id=1, source_target_pairs={{0,1},{1,2},{2,3},{4,5},{5,6},{6,7},{8,9},{9,10},{10,11},{12,13},{... | collective-permute-start | bytes 4088 | tf_op jit(solution)/shard_map/ppermute | solution.py:21
  168.1 78.0 %collective-permute-start.22 = (f32[10,34,1]{2,1,0:T(8,128)}, f32[10,34,1]{2,1,0:T(8,128)}, u32[]{:S(2)}, u32[]{:S(2)}) collective-permute-start(f32[10,34,1]{2,1,0:T(8,128)} %get-tuple-element.97), channel_id=1, source_target_pairs={{1,0},{2,1},{3,2},{5,4},{6,5},{7,6},{9,8},{10,9},{11,10},{13,12},{... | collective-permute-start | bytes 4088 | tf_op jit(solution)/shard_map/ppermute | solution.py:22
  175.3 13.3 %collective-permute-start.16 = (f32[18,66,1]{1,0,2:T(8,128)S(1)}, f32[18,66,1]{1,0,2:T(8,128)S(1)}, u32[]{:S(2)}, u32[]{:S(2)}) collective-permute-start(f32[18,66,1]{1,0,2:T(8,128)S(1)} %get-tuple-element.43), channel_id=1, source_target_pairs={{1,0},{2,1},{3,2},{5,4},{6,5},{7,6},{9,8},{10,9},{11,10},{13,12},{... | collective-permute-start | bytes 14264 | tf_op jit(solution)/shard_map/ppermute | solution.py:22
  248.7 14.6 %collective-permute-start.25 = (f32[1,32,64]{2,1,0:T(8,128)}, f32[1,32,64]{2,1,0:T(8,128)}, u32[]{:S(2)}, u32[]{:S(2)}) collective-permute-start(f32[1,32,64]{2,1,0:T(8,128)} %get-tuple-element.114), channel_id=1, source_target_pairs={{0,16},{1,17},{2,18},{3,19},{4,20},{5,21},{6,22},{7,23},{8,24},{9,... | collective-permute-start | bytes 24584 | tf_op jit(solution)/shard_map/ppermute | solution.py:21
  275.5 16.4 %collective-permute-start.28 = (f32[10,34,1]{2,1,0:T(8,128)}, f32[10,34,1]{2,1,0:T(8,128)}, u32[]{:S(2)}, u32[]{:S(2)}) collective-permute-start(f32[10,34,1]{2,1,0:T(8,128)} %get-tuple-element.94), channel_id=1, source_target_pairs={{1,0},{2,1},{3,2},{5,4},{6,5},{7,6},{9,8},{10,9},{11,10},{13,12},{... | collective-permute-start | bytes 4088 | tf_op jit(solution)/shard_map/ppermute | solution.py:22
  276.7 15.1 %collective-permute-start.29 = (f32[10,34,1]{2,1,0:T(8,128)}, f32[10,34,1]{2,1,0:T(8,128)}, u32[]{:S(2)}, u32[]{:S(2)}) collective-permute-start(f32[10,34,1]{2,1,0:T(8,128)} %get-tuple-element.95), channel_id=1, source_target_pairs={{0,1},{1,2},{2,3},{4,5},{5,6},{6,7},{8,9},{9,10},{10,11},{12,13},{... | collective-permute-start | bytes 4088 | tf_op jit(solution)/shard_map/ppermute | solution.py:21
  282.3 17.6 %collective-permute-start.37 = (f32[1,16,32]{2,1,0:T(8,128)}, f32[1,16,32]{2,1,0:T(8,128)}, u32[]{:S(2)}, u32[]{:S(2)}) collective-permute-start(f32[1,16,32]{2,1,0:T(8,128)} %get-tuple-element.156), channel_id=1, source_target_pairs={{0,16},{1,17},{2,18},{3,19},{4,20},{5,21},{6,22},{7,23},{8,24},{9,... | collective-permute-start | bytes 6152 | tf_op jit(solution)/shard_map/ppermute | solution.py:21
  320.5 16.3 %collective-permute-start.41 = (f32[6,18,1]{2,1,0:T(8,128)}, f32[6,18,1]{2,1,0:T(8,128)}, u32[]{:S(2)}, u32[]{:S(2)}) collective-permute-start(f32[6,18,1]{2,1,0:T(8,128)} %get-tuple-element.126), channel_id=1, source_target_pairs={{0,1},{1,2},{2,3},{4,5},{5,6},{6,7},{8,9},{9,10},{10,11},{12,13},{... | collective-permute-start | bytes 1304 | tf_op jit(solution)/shard_map/ppermute | solution.py:21
  357.2 12.9 %collective-permute-start.46 = (f32[6,18,1]{2,1,0:T(8,128)}, f32[6,18,1]{2,1,0:T(8,128)}, u32[]{:S(2)}, u32[]{:S(2)}) collective-permute-start(f32[6,18,1]{2,1,0:T(8,128)} %get-tuple-element.124), channel_id=1, source_target_pairs={{1,0},{2,1},{3,2},{5,4},{6,5},{7,6},{9,8},{10,9},{11,10},{13,12},{... | collective-permute-start | bytes 1304 | tf_op jit(solution)/shard_map/ppermute | solution.py:22
  364.0 13.3 %collective-permute-start.55 = (f32[1,8,16]{2,1,0:T(8,128)}, f32[1,8,16]{2,1,0:T(8,128)}, u32[]{:S(2)}, u32[]{:S(2)}) collective-permute-start(f32[1,8,16]{2,1,0:T(8,128)} %get-tuple-element.194), channel_id=1, source_target_pairs={{0,16},{1,17},{2,18},{3,19},{4,20},{5,21},{6,22},{7,23},{8,24},{9,... | collective-permute-start | bytes 1544 | tf_op jit(solution)/shard_map/ppermute | solution.py:21
  426.3 18.4 %collective-permute-start.75 = (f32[3,1,8]{2,1,0:T(1,128)S(1)}, f32[3,1,8]{2,1,0:T(1,128)S(1)}, u32[]{:S(2)}, u32[]{:S(2)}) collective-permute-start(f32[3,1,8]{2,1,0:T(1,128)S(1)} %get-tuple-element.210), channel_id=1, source_target_pairs={{0,4},{4,8},{8,12},{1,5},{5,9},{9,13},{2,6},{6,10},{10,14},{3,7},{... | collective-permute-start | bytes 296 | tf_op jit(solution)/shard_map/ppermute | solution.py:21
  455.4 15.0 %collective-permute-start.77 = (f32[3,6,1]{2,1,0:T(8,128)}, f32[3,6,1]{2,1,0:T(8,128)}, u32[]{:S(2)}, u32[]{:S(2)}) collective-permute-start(f32[3,6,1]{2,1,0:T(8,128)} %get-tuple-element.182), channel_id=1, source_target_pairs={{0,1},{1,2},{2,3},{4,5},{5,6},{6,7},{8,9},{9,10},{10,11},{12,13},{... | collective-permute-start | bytes 224 | tf_op jit(solution)/shard_map/ppermute | solution.py:21
  817.3 13.3 %collective-permute-start.160 = (f32[18,66,1]{1,0,2:T(8,128)S(1)}, f32[18,66,1]{1,0,2:T(8,128)S(1)}, u32[]{:S(2)}, u32[]{:S(2)}) collective-permute-start(f32[18,66,1]{1,0,2:T(8,128)S(1)} %get-tuple-element.41), channel_id=1, source_target_pairs={{1,0},{2,1},{3,2},{5,4},{6,5},{7,6},{9,8},{10,9},{11,10},{13,12},{... | collective-permute-start | bytes 14264 | tf_op jit(solution)/shard_map/ppermute | solution.py:22
  859.8 12.9 %collective-permute-start.166 = (f32[18,66,1]{1,0,2:T(8,128)S(1)}, f32[18,66,1]{1,0,2:T(8,128)S(1)}, u32[]{:S(2)}, u32[]{:S(2)}) collective-permute-start(f32[18,66,1]{1,0,2:T(8,128)S(1)} %get-tuple-element.39), channel_id=1, source_target_pairs={{1,0},{2,1},{3,2},{5,4},{6,5},{7,6},{9,8},{10,9},{11,10},{13,12},{... | collective-permute-start | bytes 14264 | tf_op jit(solution)/shard_map/ppermute | solution.py:22
  901.8 12.8 %collective-permute-start.172 = (f32[18,66,1]{1,0,2:T(8,128)S(1)}, f32[18,66,1]{1,0,2:T(8,128)S(1)}, u32[]{:S(2)}, u32[]{:S(2)}) collective-permute-start(f32[18,66,1]{1,0,2:T(8,128)S(1)} %get-tuple-element.37), channel_id=1, source_target_pairs={{1,0},{2,1},{3,2},{5,4},{6,5},{7,6},{9,8},{10,9},{11,10},{13,12},{... | collective-permute-start | bytes 14264 | tf_op jit(solution)/shard_map/ppermute | solution.py:22
  (204 other events, 2233.8 us)
where the time goes:
time: 942 us; the launch traced here: 925 us
  starting transfers between devices  456 us (48%)
  local copies, waits for them, and re-layouts  198 us (21%)
  other arithmetic  144 us (15%)
  waiting for transfers between devices  123 us (13%)
    ppermute x87, starting transfers between devices, extended(): before = lax.ppermute(last, axis, up)  325 us
    ppermute x87, starting transfers between devices, extended(): after = lax.ppermute(initial, axis, down)  131 us
    ppermute x87, waiting for transfers between devices, extended(): after = lax.ppermute(initial, axis, down)  109 us
    reshape x4, local copies, waits for them, and re-layouts, coarsen_sum(): values.reshape(size_x // 2, 2, size_y // 2, 2, size_z // 2, 2)  79.7 us
    unnamed x127, local copies, waits for them, and re-layouts  44.6 us
    reduce_sum x10, other arithmetic, coarsen_sum(): values.reshape(size_x // 2, 2, size_y // 2, 2, size_z // 2, 2)  39.9 us
    concatenate x63, other arithmetic, extended(): shard = jnp.concatenate([before, shard, after], axis=dim)  35.4 us
    add x19, other arithmetic, smooth_level(): iterate = iterate + OMEGA * (source - applied) / diagonal  33.4 us
  transfers between devices with their start and end apart: 174, of which 53 were waited for; matrix products, arithmetic and copies ran while one was open for 26% of the time, Pallas kernels for 0%

commit v1 on v0

v1 whole, which is shorter than its diff:
```python
import functools
import jax
import jax.numpy as jnp
from jax import lax
from jax.experimental import pallas as pl
from jax.experimental.pallas import tpu as pltpu
from jax.sharding import PartitionSpec as P

NU = 2
COARSE_SWEEPS = 8
OMEGA = 0.8
LANES = 128
PAD = 8
AXES = ("dom", "gy", "gz")
MESH = pl.DeviceIdType.MESH
F32 = jnp.float32
HI = lax.Precision.HIGHEST
UNROLL = 2


def loop(n, body, init=None, unroll=UNROLL):
    unroll = min(unroll, n)
    if init is None:
        lax.fori_loop(0, n, lambda i, c: (body(i), c)[1], 0, unroll=unroll)
        return None
    return lax.fori_loop(0, n, body, init, unroll=unroll)


def lane_index(rows):
    return lax.broadcasted_iota(jnp.int32, (rows, LANES), 1)


def pair_sum_matrix(nz):
    row = lax.broadcasted_iota(jnp.int32, (LANES, LANES), 0)
    col = lax.broadcasted_iota(jnp.int32, (LANES, LANES), 1)
    return jnp.where((row // 2 == col) & (row < nz), 1.0, 0.0).astype(F32)


def pair_copy_matrix(nz):
    row = lax.broadcasted_iota(jnp.int32, (LANES, LANES), 0)
    col = lax.broadcasted_iota(jnp.int32, (LANES, LANES), 1)
    return jnp.where((col // 2 == row) & (col < nz), 1.0, 0.0).astype(F32)


class Plan:
    def __init__(self, sizes, local):
        self.sizes = sizes
        self.names = []
        self.shapes = []
        nx, ny, nz = local
        self.local = local
        self.dims = {0: (nx, ny, nz), 1: (nx // 2, ny // 2, nz // 2)}
        self.piece = (nx // 4, ny // 4, nz // 4)
        for level in (2, 3, 4):
            s = 2**level
            self.dims[level] = tuple(d * n // s for d, n in zip(sizes, local))
        assert self.dims[2][2] <= LANES and self.piece[0] * self.piece[2] <= LANES
        self.rounds = 0
        for level in range(5):
            x, y, z = self.dims[level]
            fields = {0: "KABCDE", 1: "KABCDE", 2: "KABCDE", 3: "KABCDE", 4: "KAB"}[level]
            for field in fields:
                self.add("v%d%s" % (level, field), (x + 2, y + 2 * PAD, LANES))
            self.add("w%d" % level, (6, x, y, LANES))
            for field in "dqg":
                self.add("%s%d" % (field, level), (x, y, LANES))
            if level < 4:
                self.add("t%d" % level, (x // 2, y, LANES))
            if level < 2:
                for field in "KABCDE":
                    self.add("zs%d%s" % (level, field), (2, y, LANES))
                    self.add("zr%d%s" % (level, field), (2, y, LANES))
        for field in "KF":
            self.add("gb" + field, tuple(sizes) + (self.piece[1], LANES))
        self.sem_base = len(self.shapes)
        self.exchanges = {(l, c): i for i, (l, c) in enumerate(
            [(0, "K"), (1, "K"), (0, "A"), (0, "B"), (1, "A"), (1, "B"),
             (1, "C"), (1, "D"), (0, "C"), (0, "D"), (0, "E")])}
        n = len(self.exchanges)
        peers = max(sizes)
        self.names += ["es", "er", "gs", "gr"]
        self.shapes += [pltpu.SemaphoreType.DMA((n, 6)), pltpu.SemaphoreType.DMA((n, 6)),
                        pltpu.SemaphoreType.DMA((6, peers)), pltpu.SemaphoreType.DMA((6, peers))]

    def add(self, name, shape):
        self.names.append(name)
        self.shapes.append(pltpu.VMEM(shape, F32))


def kernel(plan, f_ref, k_ref, sol_ref, res_ref, *scratch):
    ref = dict(zip(plan.names, scratch))
    sizes = plan.sizes
    me = [lax.axis_index(a) for a in AXES]

    def copies(level, field):
        x, y, z = plan.dims[level]
        v = ref["v%d%s" % (level, field)]
        zs, zr = ref["zs%d%s" % (level, field)], ref["zr%d%s" % (level, field)]
        rnd = plan.exchanges[(level, field)]
        rows, planes = pl.ds(PAD, y), pl.ds(1, x)
        ends = [
            (v.at[x, rows], v.at[0, rows]), (v.at[1, rows], v.at[x + 1, rows]),
            (v.at[planes, pl.ds(PAD + y - 1, 1)], v.at[planes, pl.ds(PAD - 1, 1)]),
            (v.at[planes, pl.ds(PAD, 1)], v.at[planes, pl.ds(PAD + y, 1)]),
            (zs.at[1], zr.at[0]), (zs.at[0], zr.at[1]),
        ]
        result = []
        for i, (src, dst) in enumerate(ends):
            axis, up = i // 2, i % 2 == 0
            n, at = sizes[axis], me[axis]
            to = lax.rem(at + 1, n) if up else lax.rem(at + n - 1, n)
            copy = pltpu.make_async_remote_copy(
                src_ref=src, dst_ref=dst, send_sem=ref["es"].at[rnd, i], recv_sem=ref["er"].at[rnd, i],
                device_id={AXES[axis]: to}, device_id_type=MESH)
            sends = at < n - 1 if up else at > 0
            gets = at > 0 if up else at < n - 1
            result.append((copy, sends, gets))
        return result

    def start(level, field):
        for copy, sends, _ in copies(level, field):
            pl.when(sends)(copy.start)

    def finish(level, field):
        for copy, _, gets in copies(level, field):
            pl.when(gets)(copy.wait_recv)

    def drain(level, field):
        for copy, sends, _ in copies(level, field):
            pl.when(sends)(copy.wait_send)

    def zero_edges(level, field):
        x, y, z = plan.dims[level]
        v = ref["v%d%s" % (level, field)]
        zr = ref["zr%d%s" % (level, field)]
        spots = [v.at[0], v.at[x + 1], v.at[pl.ds(0, x + 2), pl.ds(0, PAD)],
                 v.at[pl.ds(0, x + 2), pl.ds(PAD + y, PAD)], zr.at[0], zr.at[1]]
        for i, spot in enumerate(spots):
            edge = me[i // 2] == (0 if i % 2 == 0 else sizes[i // 2] - 1)

            @pl.when(edge)
            def _():
                spot[...] = jnp.zeros(spot.shape, F32)

    def gather_copies(field, stage):
        gb = ref["gb" + field]
        axis = 2 - stage
        n, at = sizes[axis], me[axis]
        base = (0 if field == "K" else 3) + stage
        result = []
        for s in range(1, n):
            to, frm = lax.rem(at + s, n), lax.rem(at + n - s, n)
            index = tuple(me[: axis + 1])
            other = tuple(me[:axis]) + (frm,)
            make = functools.partial(
                pltpu.make_async_remote_copy, send_sem=ref["gs"].at[base, s], recv_sem=ref["gr"].at[base, s],
                device_id={AXES[axis]: to}, device_id_type=MESH)
            result.append((make(src_ref=gb.at[index], dst_ref=gb.at[index]),
                           make(src_ref=gb.at[other], dst_ref=gb.at[other])))
        return result

    def gather_start(field, stage):
        for out, _ in gather_copies(field, stage):
            out.start()

    def gather_finish(field, stage):
        for _, into in gather_copies(field, stage):
            into.wait_recv()

    def gather_drain(field, stage):
        for out, _ in gather_copies(field, stage):
            out.wait_send()

    def shifted(level, field, i):
        x, y, z = plan.dims[level]
        v = ref["v%d%s" % (level, field)]
        lane = lane_index(y)
        mid = v[i + 1, pl.ds(PAD, y), :]
        zp = pltpu.roll(mid, LANES - 1, 1)
        zm = pltpu.roll(mid, 1, 1)
        if level < 2:
            zr = ref["zr%d%s" % (level, field)]
            zp = jnp.where(lane == z - 1, pltpu.roll(zr[1], lax.rem(LANES + z - 1 - i, LANES), 1), zp)
            zm = jnp.where(lane == 0, pltpu.roll(zr[0], lax.rem(LANES - i, LANES), 1), zm)
        return mid, (v[i + 2, pl.ds(PAD, y), :], v[i, pl.ds(PAD, y), :],
                     v[i + 1, pl.ds(PAD + 1, y), :], v[i + 1, pl.ds(PAD - 1, y), :], zp, zm)

    def total(level, field, i):
        w = ref["w%d" % level]
        mid, beside = shifted(level, field, i)
        parts = [w[j, i] * b for j, b in enumerate(beside)]
        g = ref["g%d" % level][i]
        return mid, ((parts[0] + parts[1]) + (parts[2] + parts[3])) + ((parts[4] + parts[5]) + g)

    def fill(level, field, plane):
        x, y, z = plan.dims[level]
        v = ref["v%d%s" % (level, field)]
        if level < 2 and (level, field) in plan.exchanges:
            lane = lane_index(y)

            def body(i, carry):
                low, high = carry
                value = plane(i)
                v[i + 1, pl.ds(PAD, y), :] = value
                low = jnp.where(lane == i, jnp.broadcast_to(value[:, 0:1], (y, LANES)), low)
                high = jnp.where(lane == i, jnp.broadcast_to(value[:, z - 1:z], (y, LANES)), high)
                return low, high

            zero = jnp.zeros((y, LANES), F32)
            low, high = loop(x, body, (zero, zero))
            zs = ref["zs%d%s" % (level, field)]
            zs[0] = low
            zs[1] = high
        else:
            def body(i):
                v[i + 1, pl.ds(PAD, y), :] = plane(i)

            loop(x, body)

    def sweep(level, src, dst):
        def plane(i):
            mid, t = total(level, src, i)
            return (1.0 - OMEGA) * mid + t

        fill(level, dst, plane)

    def prepare(level):
        x, y, z = plan.dims[level]
        lane = lane_index(y)
        inside = lane < z
        w, d, q = ref["w%d" % level], ref["d%d" % level], ref["q%d" % level]

        def body(i):
            mid, beside = shifted(level, "K", i)
            beside = list(beside)
            if level >= 2:
                beside[4] = jnp.where(lane == z - 1, 0.0, beside[4])
                beside[5] = jnp.where(lane == 0, 0.0, beside[5])
            faces = [0.5 * (mid + b) for b in beside]
            diag = ((faces[0] + faces[1]) + (faces[2] + faces[3])) + (faces[4] + faces[5])
            scale = jnp.where(inside, OMEGA / jnp.where(inside, diag, 1.0), 0.0)
            d[i] = diag * (1.0 / OMEGA)
            q[i] = scale
            for j, face in enumerate(faces):
                weight = face * scale
                if level >= 2 and j == 4:
                    weight = jnp.where(lane == z - 1, 0.0, weight)
                if level >= 2 and j == 5:
                    weight = jnp.where(lane == 0, 0.0, weight)
                w[j, i] = weight

        loop(x, body)

    def restrict(level, plane, factor, store):
        x, y, z = plan.dims[level]
        t = ref["t%d" % level]
        matrix = pair_sum_matrix(z)

        def body(i):
            t[i] = plane(2 * i) + plane(2 * i + 1)

        loop(x // 2, body)

        def second(i):
            rows = t[i, pl.ds(0, y // 2, stride=2), :] + t[i, pl.ds(1, y // 2, stride=2), :]
            store(i, jnp.dot(rows * factor, matrix, precision=HI, preferred_element_type=F32))

        loop(x // 2, second)

    def residual(level, field):
        d = ref["d%d" % level]

        def plane(i):
            mid, t = total(level, field, i)
            return d[i] * (t - OMEGA * mid)

        return plane

    def correct(level, coarse):
        x, y, z = plan.dims[level]
        t = ref["t%d" % level]
        matrix = pair_copy_matrix(z)

        def body(i):
            rows = jnp.dot(coarse(i), matrix, precision=HI, preferred_element_type=F32)
            t[i, pl.ds(0, y // 2, stride=2), :] = rows
            t[i, pl.ds(1, y // 2, stride=2), :] = rows

        loop(x // 2, body)
        vb = ref["v%dB" % level]
        fill(level, "C", lambda i: vb[i + 1, pl.ds(PAD, y), :] + t[i // 2])

    px, py, pz = plan.piece

    def pack(pieces):
        whole = pieces[0]
        for i in range(1, px):
            whole = whole + pltpu.roll(pieces[i], i * pz, 1)
        return whole

    def unpack(field, store):
        gb = ref["gb" + field]
        lane = lane_index(py)
        for a in range(sizes[0]):
            for b in range(sizes[1]):
                for i in range(px):
                    rows = jnp.zeros((py, LANES), F32)
                    for c in range(sizes[2]):
                        part = gb[a, b, c]
                        shift = (pz * (c - i)) % LANES
                        if shift:
                            part = pltpu.roll(part, shift, 1)
                        rows = jnp.where(lane // pz == c, part, rows)
                    store(a * px + i, b * py, rows)

    def interior(level, field):
        x, y, z = plan.dims[level]
        v = ref["v%d%s" % (level, field)]

        def store(i, rows):
            v[i + 1, pl.ds(PAD, y), :] = rows

        return store

    def source(level):
        x, y, z = plan.dims[level]
        g, q = ref["g%d" % level], ref["q%d" % level]

        def store(i, rows):
            g[i] = q[i] * rows

        return store

    for level, field in plan.exchanges:
        zero_edges(level, field)
    barrier = pltpu.get_barrier_semaphore()
    for axis in range(3):
        for s in range(1, sizes[axis]):
            pl.semaphore_signal(barrier, inc=1, device_id={AXES[axis]: lax.rem(me[axis] + s, sizes[axis])},
                                device_id_type=MESH)

    k_plane = lambda i: k_ref[i]
    fill(0, "K", k_plane)
    restrict(0, k_plane, 0.125, interior(1, "K"))
    k1 = ref["v1K"]
    y1 = plan.dims[1][1]
    k1_plane = lambda i: k1[i + 1, pl.ds(PAD, y1), :]
    fill(1, "K", k1_plane)

    pl.semaphore_wait(barrier, sum(sizes) - 3)
    start(0, "K")
    start(1, "K")

    def own_piece(level_plane, factor, field):
        t = ref["t0"]

        def store(i, rows):
            t[i, pl.ds(0, py), :] = rows

        restrict(1, level_plane, factor, store)
        ref["gb" + field][me[0], me[1], me[2]] = pack([t[i, pl.ds(0, py), :] for i in range(px)])

    own_piece(k1_plane, 0.125, "K")
    gather_start("K", 0)
    for level in (2, 3, 4):
        x, y, z = plan.dims[level]
        for field in ("KAB" if level == 4 else "KABCDE"):
            v = ref["v%d%s" % (level, field)]
            v[0] = jnp.zeros(v.shape[1:], F32)
            v[x + 1] = jnp.zeros(v.shape[1:], F32)
            v[:, pl.ds(0, PAD), :] = jnp.zeros((x + 2, PAD, LANES), F32)
            v[:, pl.ds(PAD + y, PAD), :] = jnp.zeros((x + 2, PAD, LANES), F32)

    finish(0, "K")
    prepare(0)
    g0, q0 = ref["g0"], ref["q0"]

    def first(i):
        value = q0[i] * f_ref[i]
        g0[i] = value
        return value

    fill(0, "A", first)
    start(0, "A")
    finish(1, "K")
    prepare(1)
    gather_finish("K", 0)
    gather_start("K", 1)
    finish(0, "A")
    sweep(0, "A", "B")
    start(0, "B")
    gather_finish("K", 1)
    gather_start("K", 2)
    finish(0, "B")
    restrict(0, residual(0, "B"), 0.5, source(1))
    g1 = ref["g1"]
    fill(1, "A", lambda i: g1[i])
    start(1, "A")

    gather_finish("K", 2)
    v2k = ref["v2K"]

    def store_k(i, row, rows):
        v2k[i + 1, pl.ds(PAD + row, py), :] = rows

    unpack("K", store_k)
    for level in (2, 3):
        v, y = ref["v%dK" % level], plan.dims[level][1]
        restrict(level, lambda i: v[i + 1, pl.ds(PAD, y), :], 0.125, interior(level + 1, "K"))
    for level in (2, 3, 4):
        prepare(level)

    finish(1, "A")
    sweep(1, "A", "B")
    start(1, "B")
    finish(1, "B")
    own_piece(residual(1, "B"), 0.5, "F")
    for stage in range(3):
        gather_start("F", stage)
        gather_finish("F", stage)

    g2, q2 = ref["g2"], ref["q2"]

    def store_f(i, row, rows):
        g2[i, pl.ds(row, py), :] = q2[i, pl.ds(row, py), :] * rows

    unpack("F", store_f)
    for level in (2, 3):
        g = ref["g%d" % level]
        fill(level, "A", lambda i: g[i])
        sweep(level, "A", "B")
        restrict(level, residual(level, "B"), 0.5, source(level + 1))
    g4 = ref["g4"]
    fill(4, "A", lambda i: g4[i])
    at, other = "A", "B"
    for _ in range(COARSE_SWEEPS - 1):
        sweep(4, at, other)
        at, other = other, at
    coarse = "v4" + at
    for level in (3, 2):
        v, y = ref[coarse], plan.dims[level + 1][1]
        correct(level, lambda i: v[i + 1, pl.ds(PAD, y), :])
        sweep(level, "C", "D")
        sweep(level, "D", "E")
        coarse = "v%dE" % level

    e2 = ref["v2E"]

    def own_e2(i):
        rows = e2[me[0] * px + i + 1, pl.ds(pl.multiple_of(PAD + me[1] * py, 8), py), :]
        return pltpu.roll(rows, lax.rem(LANES - me[2] * pz, LANES), 1)

    correct(1, own_e2)
    start(1, "C")
    finish(1, "C")
    sweep(1, "C", "D")
    start(1, "D")
    finish(1, "D")
    sweep(1, "D", "E")
    e1 = ref["v1E"]
    correct(0, lambda i: e1[i + 1, pl.ds(PAD, y1), :])
    start(0, "C")
    finish(0, "C")
    sweep(0, "C", "D")
    start(0, "D")
    finish(0, "D")
    sweep(0, "D", "E")
    start(0, "E")
    y0 = plan.dims[0][1]
    e0 = ref["v0E"]

    def out(i):
        sol_ref[i] = e0[i + 1, pl.ds(PAD, y0), :]

    loop(plan.dims[0][0], out)
    finish(0, "E")
    rest = residual(0, "E")

    def last(i):
        res_ref[i] = rest(i)

    loop(plan.dims[0][0], last)

    for level, field in plan.exchanges:
        drain(level, field)
    for field in "KF":
        for stage in range(3):
            gather_drain(field, stage)


def solution(mesh):
    sizes = tuple(mesh.shape[a] for a in AXES)
    spec = P(*AXES)

    def body(right_side, coefficient):
        plan = Plan(sizes, right_side.shape)
        block = jax.ShapeDtypeStruct(right_side.shape, F32)
        vmem = pl.BlockSpec(memory_space=pltpu.VMEM)
        return pl.pallas_call(
            functools.partial(kernel, plan),
            out_shape=(block, block),
            in_specs=[vmem, vmem],
            out_specs=(vmem, vmem),
            scratch_shapes=plan.shapes,
            compiler_params=pltpu.CompilerParams(
                collective_id=0, has_side_effects=True, vmem_limit_bytes=48 * 2**20),
        )(right_side, coefficient)

    return jax.shard_map(body, mesh=mesh, in_specs=(spec, spec), out_specs=(spec, spec), check_vma=False)
```

time: 942 us -> 74.5 us (0.08)
  the two profiles are of different devices: /device:TPU:1 before, /device:TPU:0 now
where the time goes in v1:
time: 74.5 us; the launch traced here: 74.3 us
  Pallas kernels  69.9 us (94%)
  local copies, waits for them, and re-layouts  3.66 us (5%)
    pallas_call x1, Pallas kernels, body(): pl.pallas_call(functools.partial(kernel, plan), out_shape=(block, block),...  69.9 us
    unnamed x6, local copies, waits for them, and re-layouts  3.66 us

profile of v1, /device:TPU:0, one launch (start us, length us, event | category | flops | bytes accessed | tf_op | source)
XLA Modules:
  0.0 74.3 jit_solution(869784451964088903)
XLA Ops:
  0.6 0.0 copy-start
  0.6 1.0 %copy-done = f32[16,64,128]{2,1,0:T(8,128)S(1)} copy-done((f32[16,64,128]{2,1,0:T(8,128)S(1)}, f32[16,64,128]{2,1,0:T(8,128)}, u32[]{:S(2)}) %copy-start) | copy-done | bytes 524312
  1.7 0.0 copy-start.1
  1.7 1.0 %copy-done.1 = f32[16,64,128]{2,1,0:T(8,128)S(1)} copy-done((f32[16,64,128]{2,1,0:T(8,128)S(1)}, f32[16,64,128]{2,1,0:T(8,128)}, u32[]{:S(2)}) %copy-start.1) | copy-done | bytes 524312
  2.7 69.9 %shard_map.41 = (f32[16,64,128]{2,1,0:T(8,128)S(1)}, f32[16,64,128]{2,1,0:T(8,128)S(1)}) custom-call(f32[16,64,128]{2,1,0:T(8,128)S(1)} %copy-done, f32[16,64,128]{2,1,0:T(8,128)S(1)} %copy-done.1), custom_call_target="tpu_custom_call" | custom-call | tf_op jit(solution)/shard_map/pallas_call | solution.py:499
  72.7 0.8 %copy.6 = f32[16,64,128]{2,1,0:T(8,128)} copy(f32[16,64,128]{2,1,0:T(8,128)S(1)} %get-tuple-element.4) | data formatting | bytes 1048576
  73.5 0.8 %copy.7 = f32[16,64,128]{2,1,0:T(8,128)} copy(f32[16,64,128]{2,1,0:T(8,128)S(1)} %get-tuple-element.5) | data formatting | bytes 1048576
Async XLA Ops:
  0.6 1.0 %copy-start = (f32[16,64,128]{2,1,0:T(8,128)S(1)}, f32[16,64,128]{2,1,0:T(8,128)}, u32[]{:S(2)}) copy-start(f32[16,64,128]{2,1,0:T(8,128)} %f_ref.1) | copy-start | bytes 1572868
  1.7 1.0 %copy-start.1 = (f32[16,64,128]{2,1,0:T(8,128)S(1)}, f32[16,64,128]{2,1,0:T(8,128)}, u32[]{:S(2)}) copy-start(f32[16,64,128]{2,1,0:T(8,128)} %k_ref.1) | copy-start | bytes 1572868

commit v2 on v1

--- a/solution.py
+++ b/solution.py
@@ -15,7 +15,7 @@
 MESH = pl.DeviceIdType.MESH
 F32 = jnp.float32
 HI = lax.Precision.HIGHEST
-UNROLL = 2
+UNROLL = 16
 
 
 def loop(n, body, init=None, unroll=UNROLL):
@@ -77,10 +77,10 @@
             [(0, "K"), (1, "K"), (0, "A"), (0, "B"), (1, "A"), (1, "B"),
              (1, "C"), (1, "D"), (0, "C"), (0, "D"), (0, "E")])}
         n = len(self.exchanges)
-        peers = max(sizes)
+        peers = max(sizes[0] * sizes[1], sizes[2])
         self.names += ["es", "er", "gs", "gr"]
         self.shapes += [pltpu.SemaphoreType.DMA((n, 6)), pltpu.SemaphoreType.DMA((n, 6)),
-                        pltpu.SemaphoreType.DMA((6, peers)), pltpu.SemaphoreType.DMA((6, peers))]
+                        pltpu.SemaphoreType.DMA((4, peers)), pltpu.SemaphoreType.DMA((4, peers))]
 
     def add(self, name, shape):
         self.names.append(name)
@@ -144,17 +144,21 @@
 
     def gather_copies(field, stage):
         gb = ref["gb" + field]
-        axis = 2 - stage
-        n, at = sizes[axis], me[axis]
-        base = (0 if field == "K" else 3) + stage
+        base = (0 if field == "K" else 2) + stage
+        x, y, z = sizes
+        if stage == 0:
+            shifts = [(0, 0, s) for s in range(1, z)]
+        else:
+            shifts = [(s, t, 0) for s in range(x) for t in range(y) if s or t]
         result = []
-        for s in range(1, n):
-            to, frm = lax.rem(at + s, n), lax.rem(at + n - s, n)
-            index = tuple(me[: axis + 1])
-            other = tuple(me[:axis]) + (frm,)
+        for j, shift in enumerate(shifts):
+            to = [lax.rem(at + s, n) for at, s, n in zip(me, shift, sizes)]
+            frm = [lax.rem(at + n - s, n) for at, s, n in zip(me, shift, sizes)]
+            depth = 3 - stage
             make = functools.partial(
-                pltpu.make_async_remote_copy, send_sem=ref["gs"].at[base, s], recv_sem=ref["gr"].at[base, s],
-                device_id={AXES[axis]: to}, device_id_type=MESH)
+                pltpu.make_async_remote_copy, send_sem=ref["gs"].at[base, j], recv_sem=ref["gr"].at[base, j],
+                device_id=tuple(to), device_id_type=MESH)
+            index, other = tuple(me[:depth]), tuple(frm[:depth])
             result.append((make(src_ref=gb.at[index], dst_ref=gb.at[index]),
                            make(src_ref=gb.at[other], dst_ref=gb.at[other])))
         return result
@@ -334,10 +338,11 @@
     for level, field in plan.exchanges:
         zero_edges(level, field)
     barrier = pltpu.get_barrier_semaphore()
-    for axis in range(3):
-        for s in range(1, sizes[axis]):
-            pl.semaphore_signal(barrier, inc=1, device_id={AXES[axis]: lax.rem(me[axis] + s, sizes[axis])},
-                                device_id_type=MESH)
+    greeted = [(a, b, 0) for a in range(sizes[0]) for b in range(sizes[1]) if a or b]
+    greeted += [(0, 0, c) for c in range(1, sizes[2])]
+    for shift in greeted:
+        to = tuple(lax.rem(at + s, n) for at, s, n in zip(me, shift, sizes))
+        pl.semaphore_signal(barrier, inc=1, device_id=to, device_id_type=MESH)
 
     k_plane = lambda i: k_ref[i]
     fill(0, "K", k_plane)
@@ -347,7 +352,7 @@
     k1_plane = lambda i: k1[i + 1, pl.ds(PAD, y1), :]
     fill(1, "K", k1_plane)
 
-    pl.semaphore_wait(barrier, sum(sizes) - 3)
+    pl.semaphore_wait(barrier, len(greeted))
     start(0, "K")
     start(1, "K")
 
@@ -389,15 +394,13 @@
     finish(0, "A")
     sweep(0, "A", "B")
     start(0, "B")
-    gather_finish("K", 1)
-    gather_start("K", 2)
     finish(0, "B")
     restrict(0, residual(0, "B"), 0.5, source(1))
     g1 = ref["g1"]
     fill(1, "A", lambda i: g1[i])
     start(1, "A")
 
-    gather_finish("K", 2)
+    gather_finish("K", 1)
     v2k = ref["v2K"]
 
     def store_k(i, row, rows):
@@ -415,7 +418,7 @@
     start(1, "B")
     finish(1, "B")
     own_piece(residual(1, "B"), 0.5, "F")
-    for stage in range(3):
+    for stage in range(2):
         gather_start("F", stage)
         gather_finish("F", stage)
 
@@ -484,7 +487,7 @@
     for level, field in plan.exchanges:
         drain(level, field)
     for field in "KF":
-        for stage in range(3):
+        for stage in range(2):
             gather_drain(field, stage)
 
 

time: 74.5 us -> 62.8 us (0.84)
  Pallas kernels: 69.9 us -> 58.3 us
    pallas_call x1, Pallas kernels: 69.9 us -> 58.3 us  [body(): pl.pallas_call(functools.partial(kernel, plan), out_shape=(block, block),...]
where the time goes in v2:
time: 62.8 us; the launch traced here: 62.6 us
  Pallas kernels  58.3 us (93%)
  local copies, waits for them, and re-layouts  3.66 us (6%)
  between operations  0.65 us (1%)
    pallas_call x1, Pallas kernels, body(): pl.pallas_call(functools.partial(kernel, plan), out_shape=(block, block),...  58.3 us
    unnamed x6, local copies, waits for them, and re-layouts  3.66 us

profile of v2, /device:TPU:0, one launch (start us, length us, event | category | flops | bytes accessed | tf_op | source)
XLA Modules:
  0.0 62.6 jit_solution(8660854196348577602)
XLA Ops:
  0.6 0.0 copy-start
  0.6 1.0 %copy-done = f32[16,64,128]{2,1,0:T(8,128)S(1)} copy-done((f32[16,64,128]{2,1,0:T(8,128)S(1)}, f32[16,64,128]{2,1,0:T(8,128)}, u32[]{:S(2)}) %copy-start) | copy-done | bytes 524312
  1.7 0.0 copy-start.1
  1.7 1.0 %copy-done.1 = f32[16,64,128]{2,1,0:T(8,128)S(1)} copy-done((f32[16,64,128]{2,1,0:T(8,128)S(1)}, f32[16,64,128]{2,1,0:T(8,128)}, u32[]{:S(2)}) %copy-start.1) | copy-done | bytes 524312
  2.7 58.3 %shard_map.41 = (f32[16,64,128]{2,1,0:T(8,128)S(1)}, f32[16,64,128]{2,1,0:T(8,128)S(1)}) custom-call(f32[16,64,128]{2,1,0:T(8,128)S(1)} %copy-done, f32[16,64,128]{2,1,0:T(8,128)S(1)} %copy-done.1), custom_call_target="tpu_custom_call" | custom-call | tf_op jit(solution)/shard_map/pallas_call | solution.py:502
  61.0 0.8 %copy.6 = f32[16,64,128]{2,1,0:T(8,128)} copy(f32[16,64,128]{2,1,0:T(8,128)S(1)} %get-tuple-element.4) | data formatting | bytes 1048576
  61.8 0.8 %copy.7 = f32[16,64,128]{2,1,0:T(8,128)} copy(f32[16,64,128]{2,1,0:T(8,128)S(1)} %get-tuple-element.5) | data formatting | bytes 1048576
Async XLA Ops:
  0.6 1.0 %copy-start = (f32[16,64,128]{2,1,0:T(8,128)S(1)}, f32[16,64,128]{2,1,0:T(8,128)}, u32[]{:S(2)}) copy-start(f32[16,64,128]{2,1,0:T(8,128)} %f_ref.1) | copy-start | bytes 1572868
  1.7 1.0 %copy-start.1 = (f32[16,64,128]{2,1,0:T(8,128)S(1)}, f32[16,64,128]{2,1,0:T(8,128)}, u32[]{:S(2)}) copy-start(f32[16,64,128]{2,1,0:T(8,128)} %k_ref.1) | copy-start | bytes 1572868

commit v3 on v2

--- a/solution.py
+++ b/solution.py
@@ -68,14 +68,16 @@
                 self.add("t%d" % level, (x // 2, y, LANES))
             if level < 2:
                 for field in "KABCDE":
-                    self.add("zs%d%s" % (level, field), (2, y, LANES))
-                    self.add("zr%d%s" % (level, field), (2, y, LANES))
+                    self.add("zs%d%s" % (level, field), (2, PAD, LANES))
+                    self.add("zr%d%s" % (level, field), (2, PAD, LANES))
+                self.add("zx%d" % level, (2, y, LANES))
+                assert y % PAD == 0 and x * (y // PAD) <= LANES
         for field in "KF":
             self.add("gb" + field, tuple(sizes) + (self.piece[1], LANES))
         self.sem_base = len(self.shapes)
         self.exchanges = {(l, c): i for i, (l, c) in enumerate(
             [(0, "K"), (1, "K"), (0, "A"), (0, "B"), (1, "A"), (1, "B"),
-             (1, "C"), (1, "D"), (0, "C"), (0, "D"), (0, "E")])}
+             (1, "D"), (0, "C"), (0, "D"), (0, "E")])}
         n = len(self.exchanges)
         peers = max(sizes[0] * sizes[1], sizes[2])
         self.names += ["es", "er", "gs", "gr"]
@@ -118,12 +120,19 @@
         return result
 
     def start(level, field):
-        for copy, sends, _ in copies(level, field):
+        made = copies(level, field)
+        for copy, sends, _ in made[4:] + made[:4]:
             pl.when(sends)(copy.start)
 
     def finish(level, field):
         for copy, _, gets in copies(level, field):
             pl.when(gets)(copy.wait_recv)
+        x, y, z = plan.dims[level]
+        zr, zx = ref["zr%d%s" % (level, field)], ref["zx%d" % level]
+        for side in range(2):
+            face = zr[side]
+            for g in range(y // PAD):
+                zx[side, pl.ds(PAD * g, PAD), :] = pltpu.roll(face, LANES - x * g, 1) if g else face
 
     def drain(level, field):
         for copy, sends, _ in copies(level, field):
@@ -183,7 +192,7 @@
         zp = pltpu.roll(mid, LANES - 1, 1)
         zm = pltpu.roll(mid, 1, 1)
         if level < 2:
-            zr = ref["zr%d%s" % (level, field)]
+            zr = ref["zx%d" % level]
             zp = jnp.where(lane == z - 1, pltpu.roll(zr[1], lax.rem(LANES + z - 1 - i, LANES), 1), zp)
             zm = jnp.where(lane == 0, pltpu.roll(zr[0], lax.rem(LANES - i, LANES), 1), zm)
         return mid, (v[i + 2, pl.ds(PAD, y), :], v[i, pl.ds(PAD, y), :],
@@ -213,8 +222,12 @@
             zero = jnp.zeros((y, LANES), F32)
             low, high = loop(x, body, (zero, zero))
             zs = ref["zs%d%s" % (level, field)]
-            zs[0] = low
-            zs[1] = high
+            for side, face in enumerate((low, high)):
+                parts = [face[PAD * g:PAD * (g + 1)] for g in range(y // PAD)]
+                parts = [pltpu.roll(p, x * g, 1) if g else p for g, p in enumerate(parts)]
+                while len(parts) > 1:
+                    parts = [sum(parts[k + 1:k + 2], parts[k]) for k in range(0, len(parts), 2)]
+                zs[side] = parts[0]
         else:
             def body(i):
                 v[i + 1, pl.ds(PAD, y), :] = plane(i)
@@ -454,8 +467,37 @@
         return pltpu.roll(rows, lax.rem(LANES - me[2] * pz, LANES), 1)
 
     correct(1, own_e2)
-    start(1, "C")
-    finish(1, "C")
+
+    x1, z1 = plan.dims[1][0], plan.dims[1][2]
+    vb, vc, t, zx = ref["v1B"], ref["v1C"], ref["t1"], ref["zx1"]
+    matrix = pair_copy_matrix(z1)
+    spread = lambda rows: jnp.dot(rows, matrix, precision=HI, preferred_element_type=F32)
+    inner = pl.ds(PAD, y1)
+    for j, (coarse_x, fine_x) in enumerate(((-1, 0), (px, x1 + 1))):
+        rows = spread(own_e2(coarse_x))
+        t[j, pl.ds(0, py, stride=2), :] = rows
+        t[j, pl.ds(1, py, stride=2), :] = rows
+        vc[fine_x, inner, :] = vb[fine_x, inner, :] + t[j]
+    shift_z = lax.rem(LANES - me[2] * pz, LANES)
+    lane = lane_index(py)
+    low, high = jnp.zeros((py, LANES), F32), jnp.zeros((py, LANES), F32)
+    for i in range(px):
+        for first_row, row, fine_y in ((0, PAD - 1, PAD - 1), (PAD + py, 0, PAD + y1)):
+            start_row = pl.multiple_of(me[1] * py + first_row, 8)
+            rows = e2[me[0] * px + i + 1, pl.ds(start_row, PAD), :]
+            rows = spread(pltpu.roll(rows, shift_z, 1))[row:row + 1]
+            for k in (2 * i + 1, 2 * i + 2):
+                vc[k, pl.ds(fine_y, 1), :] = vb[k, pl.ds(fine_y, 1), :] + rows
+        rows = own_e2(i)
+        low = jnp.where(lane // 2 == i, jnp.broadcast_to(rows[:, LANES - 1:], (py, LANES)), low)
+        beyond = pz % LANES
+        high = jnp.where(lane // 2 == i, jnp.broadcast_to(rows[:, beyond:beyond + 1], (py, LANES)), high)
+    low = jnp.where(me[2] > 0, low, 0.0)
+    high = jnp.where(me[2] < sizes[2] - 1, high, 0.0)
+    for j, rows in enumerate((low, high)):
+        t[j, pl.ds(0, py, stride=2), :] = rows
+        t[j, pl.ds(1, py, stride=2), :] = rows
+        zx[j] = zx[j] + t[j]
     sweep(1, "C", "D")
     start(1, "D")
     finish(1, "D")

time: 62.8 us -> 59.4 us (0.946)
  Pallas kernels: 58.3 us -> 54.9 us
    pallas_call x1, Pallas kernels: 58.3 us -> 54.9 us  [body(): pl.pallas_call(functools.partial(kernel, plan), out_shape=(block, block),...]
where the time goes in v3:
time: 59.4 us; the launch traced here: 59.2 us
  Pallas kernels  54.9 us (92%)
  local copies, waits for them, and re-layouts  3.66 us (6%)
  between operations  0.65 us (1%)
    pallas_call x1, Pallas kernels, body(): pl.pallas_call(functools.partial(kernel, plan), out_shape=(block, block),...  54.9 us
    unnamed x6, local copies, waits for them, and re-layouts  3.66 us

profile of v3, /device:TPU:0, one launch (start us, length us, event | category | flops | bytes accessed | tf_op | source)
XLA Modules:
  0.0 59.2 jit_solution(3591415453086730242)
XLA Ops:
  0.6 0.0 copy-start
  0.6 1.0 %copy-done = f32[16,64,128]{2,1,0:T(8,128)S(1)} copy-done((f32[16,64,128]{2,1,0:T(8,128)S(1)}, f32[16,64,128]{2,1,0:T(8,128)}, u32[]{:S(2)}) %copy-start) | copy-done | bytes 524312
  1.7 0.0 copy-start.1
  1.7 1.0 %copy-done.1 = f32[16,64,128]{2,1,0:T(8,128)S(1)} copy-done((f32[16,64,128]{2,1,0:T(8,128)S(1)}, f32[16,64,128]{2,1,0:T(8,128)}, u32[]{:S(2)}) %copy-start.1) | copy-done | bytes 524312
  2.7 54.9 %shard_map.41 = (f32[16,64,128]{2,1,0:T(8,128)S(1)}, f32[16,64,128]{2,1,0:T(8,128)S(1)}) custom-call(f32[16,64,128]{2,1,0:T(8,128)S(1)} %copy-done, f32[16,64,128]{2,1,0:T(8,128)S(1)} %copy-done.1), custom_call_target="tpu_custom_call" | custom-call | tf_op jit(solution)/shard_map/pallas_call | solution.py:544
  57.6 0.8 %copy.6 = f32[16,64,128]{2,1,0:T(8,128)} copy(f32[16,64,128]{2,1,0:T(8,128)S(1)} %get-tuple-element.4) | data formatting | bytes 1048576
  58.4 0.8 %copy.7 = f32[16,64,128]{2,1,0:T(8,128)} copy(f32[16,64,128]{2,1,0:T(8,128)S(1)} %get-tuple-element.5) | data formatting | bytes 1048576
Async XLA Ops:
  0.6 1.0 %copy-start = (f32[16,64,128]{2,1,0:T(8,128)S(1)}, f32[16,64,128]{2,1,0:T(8,128)}, u32[]{:S(2)}) copy-start(f32[16,64,128]{2,1,0:T(8,128)} %f_ref.1) | copy-start | bytes 1572868
  1.7 1.0 %copy-start.1 = (f32[16,64,128]{2,1,0:T(8,128)S(1)}, f32[16,64,128]{2,1,0:T(8,128)}, u32[]{:S(2)}) copy-start(f32[16,64,128]{2,1,0:T(8,128)} %k_ref.1) | copy-start | bytes 1572868
